TPU v7x, 256 devices: a whole 4x4x8 slice. The times are simulated.
256 devices in a mesh: scene: 8 (over x, core), leaf: 32 (over y, z).
Axes of the slice: x: 4, y: 4, z: 8, core: 2. Of those that a mesh axis runs over, the one named last changes fastest.
Arguments:
- leaves: bfloat16 [8, 256, 8, 8, 8, 128], P('scene', 'leaf'), may hold values from -6 to 6
- counts: int32 [8, 32], P('scene', 'leaf'), may hold values from 1 to 8, as said below
- nbr_owner: int32 [8, 256, 7], P('scene', 'leaf'), may hold values from 0 to 31, all different within a row; in each aligned block of 8 rows (0 to 7, 8 to 15, ..., all dimensions but the last counted through in order) at most 4 rows name the same one
- nbr_slot: int32 [8, 256, 7], P('scene', 'leaf'), may hold values from 0 to 7
- weight: bfloat16 [3456, 256], replicated, may hold values from -0.109375 to 0.109375
- cotangent: bfloat16 [8, 256, 4, 4, 4, 256], P('scene', 'leaf'), may hold values from -6 to 6
Outputs:
- output: bfloat16 [8, 256, 4, 4, 4, 256], P('scene', 'leaf')
- grad_leaves: bfloat16 [8, 256, 8, 8, 8, 128], P('scene', 'leaf')
- grad_weight: float32 [3456, 256], P('leaf')
Inputs may be any that keep to these rules, and one draw needn't show every extreme that they name: `nbr_owner`: within the rows of one device, no owner is named by more than 4 rows, and some device names one owner in exactly 4 rows. `counts`: the live slots of a device are its first ones; in every scene some device has all 8 slots live.
All inputs are finite; a program needn't handle non-finite values.
Results may differ from a plain program's by a relative error of at most 0.0031.
Values may be sent and summed in bfloat16 or wider, within the bound.
A program may use at most 64 MiB of HBM per device.

v0:
```python
import functools

import jax
import jax.numpy as jnp
import numpy as np
from jax import lax
from jax.experimental import pallas as pl
from jax.experimental.pallas import tpu as pltpu
from jax.sharding import PartitionSpec as P

MESH = pl.DeviceIdType.MESH
BF = jnp.bfloat16
F32 = jnp.float32
CODES = (1, 2, 4, 3, 5, 6, 7)
SHIFTS = tuple(range(8))
HOLD = {s: [p for p in range(8) if p & s == s] for s in SHIFTS}
FIRST = {}
_at = 0
for _s in SHIFTS:
    FIRST[_s] = _at
    _at += len(HOLD[_s])


def tap_of(parity, shift):
    t = 0
    for axis in range(3):
        if not parity >> axis & 1:
            digit = 1
        elif shift >> axis & 1:
            digit = 0
        else:
            digit = 2
        t = 3 * t + digit
    return t


ORDER = [tap_of(p, s) for s in SHIFTS for p in HOLD[s]]


def base_of(d):
    return 16 * d if d < 3 else 36 + 4 * d


def cells_of(d):
    code = CODES[d]
    ranges = [[None] if code >> axis & 1 else list(range(4)) for axis in range(3)]
    return [(i, j, k) for i in ranges[0] for j in ranges[1] for k in ranges[2]]


def tables():
    perm = np.zeros((256, 256), np.float32)
    for x in range(4):
        for y in range(8):
            for z in range(8):
                p = (x & 1) + 2 * (y & 1) + 4 * (z & 1)
                perm[p * 32 + (x >> 1) * 16 + (y >> 1) * 4 + (z >> 1), x * 64 + y * 8 + z] = 1
    face = np.zeros((128, 64), np.float32)
    spread = np.zeros((128, 64), np.float32)
    place = {}
    for x in range(4):
        for y in range(4):
            for z in range(4):
                place[(x, y, z)] = 16 * x + 4 * y + z
    for d in range(7):
        for v, cell in enumerate(cells_of(d)):
            low = [0 if c is None else c for c in cell]
            face[d * 16 + v, 16 * low[0] + 4 * low[1] + low[2]] = 1
            spread[d * 16 + v, base_of(d) + v] = 1
            place[tuple(4 if c is None else c for c in cell)] = 64 + base_of(d) + v
    shift = np.zeros((7, 64, 128), np.float32)
    for s in range(1, 8):
        for x in range(4):
            for y in range(4):
                for z in range(4):
                    goal = (x + (s & 1), y + (s >> 1 & 1), z + (s >> 2 & 1))
                    shift[s - 1, 16 * x + 4 * y + z, place[goal]] = 1
    back = np.zeros((7, 512, 256), np.float32)
    for s in range(7):
        for leaf in range(4):
            back[s, leaf * 128 : leaf * 128 + 128, leaf * 64 : leaf * 64 + 64] = shift[s].T
    return (
        perm,
        perm.T.copy(),
        face,
        face.T.copy(),
        spread,
        shift.reshape(448, 128),
        back.reshape(7 * 512, 256),
    )


def dot(a, b):
    return jnp.dot(a, b, preferred_element_type=F32)


def kernel(
    ids, leaves, cot, w_hbm, perm, permt, face, facet, spread, shift, back,
    out, gl, gw,
    wr, xc, xt, xb, e_int, e5, gcot, cf, t128, e1s, e1r, e2s, e2r, codes, codes_in, codes_sm,
    ghost, gs, gx, gwn, gwp, cbuf, xsa, xsb, xsp, xsm, xs2p, xs2m, xra, xrb, xrp, xrm, xr2p, xr2m,
    own, lsend, lrecv, fs, frecv, of,
    w_sem, sm_sem, e1_ss, e1_rs, id_ss, id_rs, e2_ss, e2_rs, c_ss, c_rs, x_ss, x_rs, l_ss, l_rs, f_ss, f_rs,
):
    ms = lax.axis_index("scene")
    ml = lax.axis_index("leaf")
    my, mz = ml // 8, ml % 8
    mx, mc = ms // 2, ms % 2
    count = ids[3, 0]

    def leaf_at(d):
        return ((my + d // 8) % 4) * 8 + (mz + d % 8) % 8

    def leaf_from(d):
        return ((my + 4 - d // 8) % 4) * 8 + (mz + 8 - d % 8) % 8

    for n, t in enumerate(ORDER):
        pltpu.make_async_copy(
            w_hbm.at[pl.ds(t * 128, 128)], wr.at[pl.ds(n * 128, 128)], w_sem
        ).start()

    barrier = pltpu.get_barrier_semaphore()

    @pl.loop(1, 32)
    def _(d):
        pl.semaphore_signal(barrier, inc=1, device_id=(ms, leaf_at(d)), device_id_type=MESH)

    @pl.loop(1, 8)
    def _(d):
        pl.semaphore_signal(barrier, inc=1, device_id=((ms + d) % 8, ml), device_id_type=MESH)

    @pl.loop(0, 8)
    def _(i):
        rows = pl.ds(pl.multiple_of(i * 64, 64), 64)
        g = jnp.where(i < count, cot[rows, :], jnp.zeros((), BF))
        gcot[rows, :] = g
        cf[pl.ds(i * 8, 8)] = dot(face[...], g).astype(BF).reshape(8, 16, 256)

    lane = lax.broadcasted_iota(jnp.int32, (1, 128), 1)

    @pl.loop(0, 32)
    def _(o):
        row = jnp.zeros((1, 128), jnp.int32)
        for k in range(4):
            e1s[o * 4 + k] = cf[ids[0, o * 4 + k]]
            row = jnp.where((lane & 63) >> 4 == k, ids[1, o * 4 + k], row)
        codes[o] = row

    pl.semaphore_wait(barrier, 38)

    def id_copy(d, to):
        return pltpu.make_async_remote_copy(
            src_ref=codes.at[to], dst_ref=codes_in.at[ml],
            send_sem=id_ss.at[d], recv_sem=id_rs.at[d],
            device_id=(ms, to), device_id_type=MESH,
        )

    def e1_copy(d, to):
        return pltpu.make_async_remote_copy(
            src_ref=e1s.at[pl.ds(to * 4, 4)],
            dst_ref=e1r.at[pl.ds(ml * 4, 4)],
            send_sem=e1_ss.at[d], recv_sem=e1_rs.at[d],
            device_id=(ms, to), device_id_type=MESH,
        )

    def e2_copy(d, to):
        return pltpu.make_async_remote_copy(
            src_ref=e2s.at[pl.ds(to * 4, 4)],
            dst_ref=e2r.at[pl.ds(ml * 4, 4)],
            send_sem=e2_ss.at[d], recv_sem=e2_rs.at[d],
            device_id=(ms, to), device_id_type=MESH,
        )

    @pl.loop(1, 32)
    def _(d):
        id_copy(d, leaf_at(d)).start()

    @pl.loop(1, 32)
    def _(d):
        e1_copy(d, leaf_at(d)).start()

    codes_in[ml] = codes[ml]
    mine = pl.ds(ml * 4, 4)
    e1r[mine] = e1s[mine]

    @pl.loop(0, 8)
    def _(i):
        at = pl.multiple_of(i * 512, 512)
        block = jnp.concatenate([leaves[pl.ds(at, 256), :], leaves[pl.ds(at + 256, 256), :]], axis=1)
        block = jnp.where(i < count, block, jnp.zeros((), BF))
        sorted_ = dot(perm[...], block).astype(BF)
        for h in range(2):
            for p in range(8):
                xc[pl.ds(pl.multiple_of(i * 64, 64) + 32 * h, 32), p * 128 : p * 128 + 128] = sorted_[
                    p * 32 : p * 32 + 32, h * 128 : h * 128 + 128
                ]

    for p in range(8):
        xt[p * 128 : p * 128 + 128, :] = xc[:, p * 128 : p * 128 + 128].T

    pltpu.make_async_copy(w_hbm, wr, w_sem).wait()

    @pl.loop(0, 2)
    def _(b):
        rows = pl.ds(pl.multiple_of(b * 256, 256), 256)
        e_int[rows, :] = dot(xc[rows, :], wr[0:1024, :])

    @pl.loop(0, 2)
    def _(g):
        rows = pl.ds(pl.multiple_of(g * 256, 256), 256)
        for s in range(1, 8):
            ps = HOLD[s]
            for first in range(0, len(ps), 2):
                pair = ps[first : first + 2]
                block = jnp.concatenate([xc[rows, p * 128 : p * 128 + 128] for p in pair], axis=1)
                moved = dot(back[(s - 1) * 512 : s * 512, :], block).astype(BF)
                at = (FIRST[s] - 8 + first) * 128
                xb[pl.ds(pl.multiple_of(g * 512, 512), 512), at : at + 128 * len(pair)] = moved

    @pl.loop(0, 4)
    def _(b):
        rows = pl.ds(pl.multiple_of(b * 256, 256), 256)
        e5[rows, :] = dot(xb[rows, :], wr[1024:3456, :])

    @pl.loop(0, 8)
    def _(i):
        at = pl.multiple_of(i * 128, 128)
        t64 = e5[pl.ds(at + 64, 64), :].astype(BF)
        t128[pl.ds(i * 8, 8)] = dot(spread[...], t64).astype(BF).reshape(8, 16, 256)

    @pl.loop(1, 32)
    def _(d):
        id_copy(d, leaf_at(d)).wait()

    to_sm = pltpu.make_async_copy(codes_in, codes_sm, sm_sem)
    to_sm.start()
    to_sm.wait()

    @pl.loop(0, 32)
    def _(r):
        for k in range(4):
            e2s[r * 4 + k] = t128[codes_sm[r, 0, k * 16]]

    e2r[mine] = e2s[mine]

    @pl.loop(1, 32)
    def _(d):
        e1_copy(d, leaf_at(d)).wait()

    @pl.loop(1, 32)
    def _(d):
        e2_copy(d, leaf_at(d)).start()

    ghost[...] = jnp.zeros_like(ghost)
    goal = lax.broadcasted_iota(jnp.int32, (512, 128), 0)

    @pl.loop(0, 16)
    def _(m):
        row = jnp.where(lane < 64, codes_in[2 * m], codes_in[2 * m + 1])
        d = row & 7
        target = (row >> 3) * 64 + jnp.where(d < 3, 16 * d, 36 + 4 * d) + (lane & 15)
        pick = jnp.where(goal == target, 1.0, 0.0).astype(BF)
        ghost[...] += dot(pick, e1r[pl.ds(m * 8, 8)].reshape(128, 256))

    gs[0:512, :] = gcot[...]

    @pl.loop(0, 8)
    def _(i):
        rows = pl.ds(pl.multiple_of(i * 64, 64), 64)
        g5 = jnp.concatenate([gcot[rows, :], ghost[rows, :].astype(BF)], axis=0)
        moved = dot(shift[...], g5).astype(BF)
        for s in range(1, 8):
            gs[pl.ds(pl.multiple_of(s * 512 + i * 64, 64), 64), :] = moved[(s - 1) * 64 : s * 64, :]

    gwn[3456:3472, :] = jnp.zeros((16, 256), F32)
    for s in SHIFTS:
        for p in HOLD[s]:
            t = tap_of(p, s)
            gwn[t * 128 : t * 128 + 128, :] = dot(
                xt[p * 128 : p * 128 + 128, :], gs[s * 512 : s * 512 + 512, :]
            )

    @pl.loop(0, 16)
    def _(m):
        at = pl.multiple_of(m * 216, 8)
        even = gwn[pl.ds(at, 112), :]
        odd = gwn[pl.ds(pl.multiple_of(at + 104, 8), 120), :][4:116, :]
        for s in range(7):
            gwp[pl.ds(pl.multiple_of(s * 512 + m * 32, 16), 16), :] = even[s * 16 : s * 16 + 16, :]
            gwp[pl.ds(pl.multiple_of(s * 512 + m * 32 + 16, 16), 16), :] = odd[s * 16 : s * 16 + 16, :]

    gwp[7 * 512 : 8 * 512, :] = jnp.zeros((512, 256), F32)

    def c_copy(n):
        cx = (mx + n) % 4
        return pltpu.make_async_remote_copy(
            src_ref=gwp.at[pl.ds(pl.multiple_of((2 * cx + 1 - mc) * 512, 512), 512)],
            dst_ref=cbuf.at[pl.ds(pl.multiple_of(cx * 512, 512), 512)],
            send_sem=c_ss.at[n], recv_sem=c_rs.at[n],
            device_id=(2 * mx + 1 - mc, ml), device_id_type=MESH,
        )

    for n in (2, 1, 3, 0):
        c_copy(n).start()

    def chip_sum(n, half):
        cx = (mx + n) % 4
        a = gwp[pl.ds(pl.multiple_of((2 * cx + mc) * 512 + half * 256, 256), 256), :]
        b = cbuf[pl.ds(pl.multiple_of(cx * 512 + half * 256, 256), 256), :]
        return a + b

    up = (2 * ((mx + 1) % 4) + mc, ml)
    down = (2 * ((mx + 3) % 4) + mc, ml)

    def x_copy(n, src, dst, to):
        return pltpu.make_async_remote_copy(
            src_ref=src, dst_ref=dst, send_sem=x_ss.at[n], recv_sem=x_rs.at[n],
            device_id=to, device_id_type=MESH,
        )

    c_copy(2).wait()
    xsa[...] = chip_sum(2, 0).astype(BF)
    xsb[...] = chip_sum(2, 1).astype(BF)
    x0 = x_copy(0, xsa, xra, up)
    x0.start()
    x1 = x_copy(1, xsb, xrb, down)
    x1.start()
    c_copy(1).wait()
    xsp[...] = chip_sum(1, 1).astype(BF)
    x2 = x_copy(2, xsp, xrp, up)
    x2.start()
    c_copy(3).wait()
    xsm[...] = chip_sum(3, 0).astype(BF)
    x3 = x_copy(3, xsm, xrm, down)
    x3.start()
    c_copy(0).wait()
    x0.wait()
    xs2p[...] = (chip_sum(1, 0) + xra[...].astype(F32)).astype(BF)
    x4 = x_copy(4, xs2p, xr2p, up)
    x4.start()
    x1.wait()
    xs2m[...] = (chip_sum(3, 1) + xrb[...].astype(F32)).astype(BF)
    x5 = x_copy(5, xs2m, xr2m, down)
    x5.start()

    @pl.loop(0, 2)
    def _(b):
        rows = pl.ds(pl.multiple_of(b * 256, 256), 256)
        for s in SHIFTS:
            ps = HOLD[s]
            first = FIRST[s] * 128
            part = lax.dot_general(
                gs[pl.ds(pl.multiple_of(s * 512 + b * 256, 256), 256), :],
                wr[first : first + 128 * len(ps), :],
                (((1,), (1,)), ((), ())),
                preferred_element_type=F32,
            )
            for n, p in enumerate(ps):
                piece = part[:, n * 128 : n * 128 + 128]
                if s == 0:
                    gx[rows, p * 128 : p * 128 + 128] = piece
                else:
                    gx[rows, p * 128 : p * 128 + 128] += piece

    @pl.loop(0, 8)
    def _(i):
        halves = []
        for h in range(2):
            rows = pl.ds(pl.multiple_of(i * 64, 64) + 32 * h, 32)
            halves.append(jnp.concatenate([gx[rows, p * 128 : p * 128 + 128] for p in range(8)], axis=0))
        block = jnp.concatenate(halves, axis=1).astype(BF)
        block = jnp.where(i < count, block, jnp.zeros((), BF))
        back_ = dot(permt[...], block).astype(BF)
        at = pl.multiple_of(i * 512, 512)
        gl[pl.ds(at, 256), :] = back_[:, 0:128]
        gl[pl.ds(at + 256, 256), :] = back_[:, 128:256]

    x3.wait()
    x4.wait()
    own[0:256, :] = chip_sum(0, 0) + xrm[...].astype(F32) + xr2p[...].astype(F32)
    x2.wait()
    x5.wait()
    own[256:512, :] = chip_sum(0, 1) + xrp[...].astype(F32) + xr2m[...].astype(F32)
    lsend[...] = own[...].astype(BF)

    def l_copy(d, to):
        return pltpu.make_async_remote_copy(
            src_ref=lsend.at[pl.ds(pl.multiple_of(to * 16, 16), 16)],
            dst_ref=lrecv.at[pl.ds(pl.multiple_of(ml * 16, 16), 16)],
            send_sem=l_ss.at[d], recv_sem=l_rs.at[d],
            device_id=(ms, to), device_id_type=MESH,
        )

    @pl.loop(1, 32)
    def _(d):
        l_copy(d, leaf_at(d)).start()

    tile = pl.ds(pl.multiple_of(ml * 16, 16), 16)
    lrecv[tile, :] = lsend[tile, :]

    @pl.loop(1, 32)
    def _(d):
        l_copy(d, leaf_at(d)).wait()

    total = jnp.zeros((16, 256), F32)
    for r in range(32):
        total = total + lrecv[r * 16 : r * 16 + 16, :].astype(F32)
    fs[...] = total

    def f_copy(d):
        return pltpu.make_async_remote_copy(
            src_ref=fs, dst_ref=frecv.at[pl.ds(pl.multiple_of(ms * 16, 16), 16)],
            send_sem=f_ss.at[d], recv_sem=f_rs.at[d],
            device_id=((ms + d) % 8, ml), device_id_type=MESH,
        )

    @pl.loop(1, 8)
    def _(d):
        f_copy(d).start()

    frecv[pl.ds(pl.multiple_of(ms * 16, 16), 16), :] = fs[...]

    @pl.loop(1, 32)
    def _(d):
        e2_copy(d, leaf_at(d)).wait()

    @pl.loop(0, 8)
    def _(i):
        for d in range(7):
            of[d * 16 : d * 16 + 16, :] = e2r[ids[2, i * 8 + d]]
        of[112:128, :] = jnp.zeros((16, 256), BF)
        rows = pl.ds(pl.multiple_of(i * 64, 64), 64)
        y = e_int[rows, :] + e5[pl.ds(pl.multiple_of(i * 128, 128), 64), :] + dot(facet[...], of[...])
        out[rows, :] = jnp.where(i < count, y, 0.0).astype(BF)

    @pl.loop(1, 8)
    def _(d):
        f_copy(d).wait()

    gw[...] = frecv[0:108, :]


def request_tables(nbr_owner, nbr_slot, counts):
    pad = ((0, 0), (0, 1))
    pick = np.array([code - 1 for code in CODES])
    owners = jnp.pad(nbr_owner[:, pick], pad, constant_values=32).reshape(64)
    blocks = (jnp.pad(nbr_slot[:, pick], pad) * 8 + jnp.arange(8, dtype=jnp.int32)[None, :]).reshape(64)
    n = jnp.arange(64, dtype=jnp.int32)
    rank = jnp.sum((owners[:, None] == owners[None, :]) & (n[None, :] < n[:, None]), axis=1, dtype=jnp.int32)
    place = owners * 4 + rank
    hit = place[None, :] == jnp.arange(128, dtype=jnp.int32)[:, None]
    source = 7 + jnp.sum(jnp.where(hit, n[None, :] - 7, 0), axis=1, dtype=jnp.int32)
    code = 7 + jnp.sum(jnp.where(hit, blocks[None, :] - 7, 0), axis=1, dtype=jnp.int32)
    places = jnp.pad(place, (0, 64))
    return jnp.stack([source, code, places, jnp.broadcast_to(counts.reshape(1), (128,))])


def per_device(leaves, counts, nbr_owner, nbr_slot, weight, cotangent):
    ids = request_tables(nbr_owner[0], nbr_slot[0], counts)
    consts = [jnp.asarray(t, BF) for t in tables()]
    vmem = pl.BlockSpec(memory_space=pltpu.VMEM)
    sems = pltpu.SemaphoreType.DMA
    V = pltpu.VMEM
    out, gl, gw = pl.pallas_call(
        kernel,
        out_shape=(
            jax.ShapeDtypeStruct((512, 256), BF),
            jax.ShapeDtypeStruct((4096, 128), BF),
            jax.ShapeDtypeStruct((108, 256), F32),
        ),
        in_specs=[pl.BlockSpec(memory_space=pltpu.SMEM), vmem, vmem, pl.BlockSpec(memory_space=pl.ANY)]
        + [vmem] * 7,
        out_specs=(vmem, vmem, vmem),
        scratch_shapes=[
            V((3456, 256), BF), V((512, 1024), BF), V((1024, 512), BF), V((1024, 2432), BF),
            V((512, 256), F32), V((1024, 256), F32), V((512, 256), BF), V((64, 16, 256), BF), V((64, 16, 256), BF),
            *[V((128, 16, 256), BF) for _ in range(4)],
            V((32, 1, 128), jnp.int32), V((32, 1, 128), jnp.int32), pltpu.SMEM((32, 1, 128), jnp.int32),
            V((512, 256), F32), V((4096, 256), BF), V((512, 1024), F32), V((3472, 256), F32),
            V((4096, 256), F32), V((2048, 256), F32),
            *[V((256, 256), BF) for _ in range(12)],
            V((512, 256), F32), V((512, 256), BF), V((512, 256), BF), V((16, 256), F32), V((128, 256), F32),
            V((128, 256), BF),
            sems, sems, sems((32,)), sems((32,)), sems((32,)), sems((32,)), sems((32,)), sems((32,)),
            sems((4,)), sems((4,)), sems((6,)), sems((6,)), sems((32,)), sems((32,)), sems((8,)), sems((8,)),
        ],
        compiler_params=pltpu.CompilerParams(
            collective_id=0, has_side_effects=True, vmem_limit_bytes=56 * 1024 * 1024
        ),
        cost_estimate=pl.CostEstimate(flops=3 * 10**9, bytes_accessed=5 * 10**6, transcendentals=0),
    )(ids, leaves.reshape(4096, 128), cotangent.reshape(512, 256), weight, *consts)
    return (
        out.reshape(1, 8, 4, 4, 4, 256),
        gl.reshape(1, 8, 8, 8, 8, 128),
        gw,
    )


def solution(mesh):
    six = P("scene", "leaf", None, None, None, None)
    return jax.shard_map(
        per_device,
        mesh=mesh,
        in_specs=(six, P("scene", "leaf"), P("scene", "leaf", None), P("scene", "leaf", None), P(), six),
        out_specs=(six, six, P("leaf", None)),
        check_vma=False,
    )
```

profile of v0, /device:TPU:1, one launch (start us, length us, event | category | flops | bytes accessed | tf_op | source)
XLA Modules:
  0.0 91.2 jit_solution(3964199470352552230)
XLA Ops:
  1.3 0.1 pad.17.clone
  1.4 0.7 pad_clamp_fusion
  2.0 0.7 copy.37
  2.7 0.6 gather_fusion
  3.3 0.1 copy.33
  3.3 0.1 reshape.70
  3.4 0.2 convert_reduce_fusion
  3.6 0.7 copy.36
  4.3 0.6 gather_fusion.1
  4.9 0.1 copy.30
  5.0 0.1 sub.10
  5.0 0.1 select_reduce_fusion.1
  5.2 0.6 add_add_fusion.1.ids
  5.8 1.7 %reshape.73.cot = bf16[512,256]{1,0:T(8,128)(2,1)} reshape(bf16[1,8,4,4,4,256]{5,4,3,2,1,0:T(4,128)(2,1)} %param.21) | data formatting | bytes 524288 | tf_op jit(solution)/shard_map/reshape | solution.py:490
  7.5 79.0 %shard_map.175 = (bf16[512,256]{1,0:T(8,128)(2,1)}, bf16[4096,128]{1,0:T(8,128)(2,1)}, f32[108,256]{1,0:T(8,128)}) custom-call(s32[4,128]{1,0:T(4,128)} %add_add_fusion.1.ids, bf16[4096,128]{1,0:T(8,128)(2,1)} %bitcast.27, bf16[512,256]{1,0:T(8,128)(2,1)} %reshape.73.cot, bf16[3456,256]{1,0:T(8,128)(2,1)} %w_hbm.1, bf16[256,256]{1,0:T(8,128)(2,1)} %constant.35.clone.perm, ...), custom_call_target="tpu_custom_call" | custom-call | flops 3000000000 | bytes 5000000 | tf_op jit(solution)/shard_map/pallas_call | solution.py:463
  86.6 0.0 copy-start
  86.6 1.8 %reshape.74 = bf16[1,8,4,4,4,256]{5,4,3,2,1,0:T(4,128)(2,1)} reshape(bf16[512,256]{1,0:T(8,128)(2,1)} %get-tuple-element.6) | data formatting | bytes 524288 | tf_op jit(solution)/shard_map/reshape | solution.py:492
  88.3 2.3 %copy.41 = bf16[1,8,8,8,8,128]{5,4,3,2,1,0:T(8,128)(2,1)} copy(bf16[1,8,8,8,8,128]{5,4,3,2,1,0:T(8,128)(2,1)} %bitcast.22) | data formatting | bytes 2097152
  90.6 0.0 copy-done
  90.6 0.6 copy.42
  (6 shorter events, 0.0 us)
Async XLA Ops:
  86.6 4.0 %copy-start = (f32[108,256]{1,0:T(8,128)S(1)}, f32[108,256]{1,0:T(8,128)}, u32[]{:S(2)}) copy-start(f32[108,256]{1,0:T(8,128)} %get-tuple-element.18) | copy-start | bytes 331780
where the time goes:
time: 91.5 us; the launch traced here: 91.2 us
  Pallas kernels  79 us (86%)
  local copies, waits for them, and re-layouts  9.26 us (10%)
  other arithmetic  1.62 us (2%)
  between operations  1.34 us (1%)
    pallas_call x1, Pallas kernels, per_device(): pl.pallas_call(kernel, out_shape=(jax.ShapeDtypeStruct((512, 256), BF), j...  79 us
    unnamed x5, local copies, waits for them, and re-layouts  2.99 us

commit v1 on v0

v1 whole, which is shorter than its diff:
```python
import functools

import jax
import jax.numpy as jnp
import numpy as np
from jax import lax
from jax.experimental import pallas as pl
from jax.experimental.pallas import tpu as pltpu
from jax.sharding import PartitionSpec as P

MESH = pl.DeviceIdType.MESH
BF = jnp.bfloat16
F32 = jnp.float32
CODES = (1, 2, 4, 3, 5, 6, 7)
SHIFTS = tuple(range(8))
CHUNK, HALFC = 448, 224
FAR_FIRST = (4, 3, 5, 2, 6, 1, 7, 0)
ROWS, PART = 304, 160
HOLD = {s: [p for p in range(8) if p & s == s] for s in SHIFTS}
FIRST = {}
_at = 0
for _s in SHIFTS:
    FIRST[_s] = _at
    _at += len(HOLD[_s])


def tap_of(parity, shift):
    t = 0
    for axis in range(3):
        if not parity >> axis & 1:
            digit = 1
        elif shift >> axis & 1:
            digit = 0
        else:
            digit = 2
        t = 3 * t + digit
    return t


ORDER = [tap_of(p, s) for s in SHIFTS for p in HOLD[s]]


def base_of(d):
    return 16 * d if d < 3 else 36 + 4 * d


def cells_of(d):
    code = CODES[d]
    ranges = [[None] if code >> axis & 1 else list(range(4)) for axis in range(3)]
    return [(i, j, k) for i in ranges[0] for j in ranges[1] for k in ranges[2]]


def tables():
    perm = np.zeros((256, 256), np.float32)
    for x in range(4):
        for y in range(8):
            for z in range(8):
                p = (x & 1) + 2 * (y & 1) + 4 * (z & 1)
                perm[p * 32 + (x >> 1) * 16 + (y >> 1) * 4 + (z >> 1), x * 64 + y * 8 + z] = 1
    facet = np.zeros((64, 128), np.float32)
    low_cells = [c for c in np.ndindex(4, 4, 4) if 0 in c]
    gather = np.zeros((ROWS, 512), np.float32)
    for leaf in range(8):
        for n, (x, y, z) in enumerate(low_cells):
            gather[leaf * 37 + n, leaf * 64 + 16 * x + 4 * y + z] = 1
    expand = np.zeros((64, 16, 384), np.float32)
    spread = np.zeros((128, 64), np.float32)
    place = {}
    for x in range(4):
        for y in range(4):
            for z in range(4):
                place[(x, y, z)] = 16 * x + 4 * y + z
    for d in range(7):
        for v, cell in enumerate(cells_of(d)):
            low = [0 if c is None else c for c in cell]
            facet[16 * low[0] + 4 * low[1] + low[2], d * 16 + v] = 1
            for leaf in range(8):
                expand[leaf * 8 + d, v, leaf * 37 + low_cells.index(tuple(low))] = 1
            spread[d * 16 + v, base_of(d) + v] = 1
            place[tuple(4 if c is None else c for c in cell)] = 64 + base_of(d) + v
    shift = np.zeros((7, 64, 128), np.float32)
    for s in range(1, 8):
        for x in range(4):
            for y in range(4):
                for z in range(4):
                    goal = (x + (s & 1), y + (s >> 1 & 1), z + (s >> 2 & 1))
                    shift[s - 1, 16 * x + 4 * y + z, place[goal]] = 1
    back = np.zeros((7, 512, 256), np.float32)
    for s in range(7):
        for leaf in range(4):
            back[s, leaf * 128 : leaf * 128 + 128, leaf * 64 : leaf * 64 + 64] = shift[s].T
    return (
        perm,
        perm.T.copy(),
        facet,
        spread,
        gather,
        expand,
        shift.reshape(448, 128),
        back.reshape(7 * 512, 256),
    )


def dot(a, b):
    return jnp.dot(a, b, preferred_element_type=F32)


def kernel(
    ids, idv, leaves_h, cot_h, w_h, perm_h, permt_h, facet_h, spread_h, gather_h, expand_h, shift_h, back_h,
    out_h, gl_h, gw,
    leaves, cot, perm, permt, facet, spread, gather, expand, shift, back, out, gl,
    wr, xc, xt, xb, e_int, e5, gcot, ub, t128, e1s, e1r, e2s, e2m, e2r, codes, codes_sm, pick,
    ghost, gs, gx, gwn, gwp, cbuf, xsa, xsb, xsp, xsm, xs2p, xs2m, xra, xrb, xrp, xrm, xr2p, xr2m,
    own, lsend, lrecv, zsend, zrecv, fs, frecv, of,
    in_sem, w_sem, sm_sem, out_sem, ag_ss, ag_rs, iz_ss, iz_rs, iy_ss, iy_rs, e1_ss, e1_rs, ea_ss, ea_rs, eb_ss, eb_rs,
    c_ss, c_rs, x_ss, x_rs, ly_ss, ly_rs, lz_ss, lz_rs, f_ss, f_rs,
):
    ms = lax.axis_index("scene")
    ml = lax.axis_index("leaf")
    my, mz = ml // 8, ml % 8
    mx, mc = ms // 2, ms % 2
    count = ids[3, 0]

    def remote(src, dst, ss, rs, to):
        return pltpu.make_async_remote_copy(
            src_ref=src, dst_ref=dst, send_sem=ss, recv_sem=rs, device_id=to, device_id_type=MESH
        )

    def at_z(d):
        return (ms, my * 8 + (mz + d) % 8)

    def at_y(d):
        return (ms, (my + d) % 4 * 8 + mz)

    loads = [
        pltpu.make_async_copy(src, dst, in_sem.at[n])
        for n, (src, dst) in enumerate(
            (
                (cot_h, cot), (gather_h, gather), (leaves_h, leaves), (perm_h, perm), (expand_h, expand),
                (back_h, back), (spread_h, spread), (shift_h, shift), (permt_h, permt), (facet_h, facet),
            )
        )
    ]
    for load in loads[:4]:
        load.start()

    for n, t in enumerate(ORDER):
        pltpu.make_async_copy(
            w_h.at[pl.ds(t * 128, 128)], wr.at[pl.ds(n * 128, 128)], w_sem
        ).start()
    for load in loads[4:]:
        load.start()

    barrier = pltpu.get_barrier_semaphore()

    @pl.loop(1, 8)
    def _(d):
        pl.semaphore_signal(barrier, inc=1, device_id=at_z(d), device_id_type=MESH)
        pl.semaphore_signal(barrier, inc=1, device_id=((ms + d) % 8, ml), device_id_type=MESH)

    @pl.loop(1, 4)
    def _(d):
        pl.semaphore_signal(barrier, inc=1, device_id=at_y(d), device_id_type=MESH)

    loads[0].wait()

    @pl.loop(0, 8)
    def _(i):
        rows = pl.ds(pl.multiple_of(i * 64, 64), 64)
        gcot[rows, :] = jnp.where(i < count, cot[rows, :], jnp.zeros((), BF))

    loads[1].wait()
    ub[mz] = dot(gather[...], gcot[...]).astype(BF)
    codes[ml, :, 0:128] = idv[0:1, :]
    codes[ml, :, 128:256] = idv[1:2, :]

    loads[2].wait()
    loads[3].wait()

    @pl.loop(0, 8)
    def _(i):
        at = pl.multiple_of(i * 512, 512)
        block = jnp.concatenate([leaves[pl.ds(at, 256), :], leaves[pl.ds(at + 256, 256), :]], axis=1)
        block = jnp.where(i < count, block, jnp.zeros((), BF))
        sorted_ = dot(perm[...], block).astype(BF)
        for h in range(2):
            for p in range(8):
                xc[pl.ds(pl.multiple_of(i * 64, 64) + 32 * h, 32), p * 128 : p * 128 + 128] = sorted_[
                    p * 32 : p * 32 + 32, h * 128 : h * 128 + 128
                ]

    pl.semaphore_wait(barrier, 17)

    halves = (pl.ds(0, PART), pl.ds(PART, ROWS - PART))

    def ag_copy(way, half, hop):
        origin = (mz + 8 - (hop - 1)) % 8 if way == 0 else (mz + hop - 1) % 8
        block = ub.at[origin, halves[half]]
        n = (way * 2 + half) * 4 + hop - 1
        return remote(block, block, ag_ss.at[n], ag_rs.at[n], at_z(1 if way == 0 else 7))

    def iz_copy(d):
        return remote(codes.at[ml], codes.at[ml], iz_ss.at[d], iz_rs.at[d], at_z(d))

    def iy_copy(d):
        group = codes.at[pl.ds(my * 8, 8)]
        return remote(group, group, iy_ss.at[d], iy_rs.at[d], at_y(d))

    @pl.loop(1, 8)
    def _(d):
        iz_copy(d).start()

    for way in range(2):
        for half in (way, 1 - way):
            ag_copy(way, half, 1).start()

    for p in range(8):
        xt[p * 128 : p * 128 + 128, :] = xc[:, p * 128 : p * 128 + 128].T

    @pl.loop(1, 8)
    def _(d):
        iz_copy(d).wait()

    for d in range(1, 4):
        iy_copy(d).start()
    group = pl.ds(my * 8, 8)
    to_sm = pltpu.make_async_copy(codes.at[group], codes_sm.at[group], sm_sem)
    to_sm.start()
    to_sm.wait()

    for load in loads[4:]:
        load.wait()

    def e1_copy(q, d):
        z = (mz + q) % 8
        to = (my + d) % 4
        return remote(
            e1s.at[pl.ds((z * 4 + to) * 4, 4)], e1r.at[pl.ds((z * 4 + my) * 4, 4)],
            e1_ss.at[q * 4 + d], e1_rs.at[q * 4 + d], at_y(d),
        )

    def serve(q):
        z = (mz + q) % 8
        picks = jnp.concatenate(
            [
                expand[codes_sm[my * 8 + z, 0, (y * 8 + mz) * 4 + k]]
                for y in range(4)
                for k in range(4)
            ],
            axis=0,
        )
        rows = dot(picks[:, 0:ROWS], ub[z]).astype(BF)
        e1s[pl.ds(z * 16, 16)] = rows.reshape(16, 16, 256)
        for d in range(1, 4):
            e1_copy(q, d).start()
        e1r[pl.ds((z * 4 + my) * 4, 4)] = e1s[pl.ds((z * 4 + my) * 4, 4)]

    serve(0)
    pltpu.make_async_copy(w_h, wr, w_sem).wait()

    @pl.loop(0, 2)
    def _(b):
        rows = pl.ds(pl.multiple_of(b * 256, 256), 256)
        e_int[rows, :] = dot(xc[rows, :], wr[0:1024, :])

    def forward_shift(g):
        rows = pl.ds(g * 256, 256)
        for s in range(1, 8):
            ps = HOLD[s]
            for first in range(0, len(ps), 2):
                pair = ps[first : first + 2]
                block = jnp.concatenate([xc[rows, p * 128 : p * 128 + 128] for p in pair], axis=1)
                moved = dot(back[(s - 1) * 512 : s * 512, :], block).astype(BF)
                at = (FIRST[s] - 8 + first) * 128
                xb[pl.ds(g * 512, 512), at : at + 128 * len(pair)] = moved

    def forward_rows(b):
        e5[pl.ds(b * 256, 256), :] = dot(xb[pl.ds(b * 256, 256), :], wr[1024:3456, :])
        for i in (2 * b, 2 * b + 1):
            t64 = e5[pl.ds(i * 128 + 64, 64), :].astype(BF)
            t128[pl.ds(i * 8, 8)] = dot(spread[...], t64).astype(BF).reshape(8, 16, 256)

    def hop_done(way, half, hop):
        ag_copy(way, half, hop).wait()
        if hop < (4 if half == way else 3):
            ag_copy(way, half, hop + 1).start()

    def hop_all(hop):
        for half in (0, 1):
            hop_done(0, half, hop)
            hop_done(1, 1 - half, hop)

    def ea_copy(q, d):
        z = (mz + q) % 8
        to = (my + d) % 4
        return remote(
            e2s.at[pl.ds((to * 8 + z) * 4, 4)], e2m.at[pl.ds((z * 4 + my) * 4, 4)],
            ea_ss.at[q * 4 + d], ea_rs.at[q * 4 + d], at_y(d),
        )

    def eb_copy(d):
        z = (mz + d) % 8
        return remote(
            e2m.at[pl.ds(z * 16, 16)], e2r.at[pl.ds(mz * 16, 16)], eb_ss.at[d], eb_rs.at[d], at_z(d)
        )

    forward_shift(0)
    hop_all(1)
    serve(7)
    serve(1)
    forward_shift(1)
    forward_rows(0)
    hop_all(2)
    serve(6)
    serve(2)
    for d in range(1, 4):
        iy_copy(d).wait()
    all_sm = pltpu.make_async_copy(codes, codes_sm, sm_sem)
    all_sm.start()
    all_sm.wait()
    forward_rows(1)
    forward_rows(2)
    hop_all(3)
    serve(5)
    serve(3)
    forward_rows(3)

    lane = lax.broadcasted_iota(jnp.int32, (1, 256), 1)
    goal = lax.broadcasted_iota(jnp.int32, (512, 256), 0)

    def make_pick(q):
        z = (mz + q) % 8
        row = jnp.zeros((1, 256), jnp.int32)
        for y in range(4):
            for k in range(4):
                row = jnp.where(lane >> 4 == y * 4 + k, codes_sm[y * 8 + z, 0, 128 + ml * 4 + k], row)
        d = row & 7
        target = (row >> 3) * 64 + jnp.where(d < 3, 16 * d, 36 + 4 * d) + (lane & 15)
        pick[q] = jnp.where(goal == target, 1.0, 0.0).astype(BF)

    ag_copy(0, 0, 4).wait()
    ag_copy(1, 1, 4).wait()
    serve(4)

    @pl.loop(0, 32)
    def _(r):
        for k in range(4):
            e2s[r * 4 + k] = t128[codes_sm[r, 0, 128 + ml * 4 + k]]

    for q in FAR_FIRST:
        for d in range(1, 4):
            ea_copy(q, d).start()
    for z in range(8):
        e2m[pl.ds((z * 4 + my) * 4, 4)] = e2s[pl.ds((my * 8 + z) * 4, 4)]

    @pl.loop(0, 8)
    def _(q):
        make_pick(q)

    for q in (0, 7, 1, 6, 2, 5, 3, 4):
        for d in range(1, 4):
            e1_copy(q, d).wait()
        z = (mz + q) % 8
        part = dot(pick[q], e1r[pl.ds(z * 16, 16)].reshape(256, 256))
        if q == 0:
            ghost[...] = part
        else:
            ghost[...] += part

    def forward_on(q):
        for d in range(1, 4):
            ea_copy(q, d).wait()
        if q:
            eb_copy(q).start()

    forward_on(4)
    gs[0:512, :] = gcot[...]

    @pl.loop(0, 8)
    def _(i):
        rows = pl.ds(pl.multiple_of(i * 64, 64), 64)
        g5 = jnp.concatenate([gcot[rows, :], ghost[rows, :].astype(BF)], axis=0)
        moved = dot(shift[...], g5).astype(BF)
        for s in range(1, 8):
            gs[pl.ds(pl.multiple_of(s * 512 + i * 64, 64), 64), :] = moved[(s - 1) * 64 : s * 64, :]

    forward_on(3)
    gwn[3456:3472, :] = jnp.zeros((16, 256), F32)
    for s in SHIFTS:
        for p in HOLD[s]:
            t = tap_of(p, s)
            gwn[t * 128 : t * 128 + 128, :] = dot(
                xt[p * 128 : p * 128 + 128, :], gs[s * 512 : s * 512 + 512, :]
            )

    forward_on(5)

    @pl.loop(0, 16)
    def _(n):
        at = pl.multiple_of(n * 216, 8)
        even = gwn[pl.ds(at, 112), :]
        odd = gwn[pl.ds(pl.multiple_of(at + 104, 8), 120), :][4:116, :]
        for h, block in ((0, even), (1, odd)):
            leaf = 2 * n + h
            for m in range(7):
                goal_at = (leaf + m) % 8 * CHUNK + leaf // 8 * 112 + (6 - m) * 16
                gwp[pl.ds(pl.multiple_of(goal_at, 16), 16), :] = block[m * 16 : m * 16 + 16, :]

    def c_copy(n):
        cx = (mx + n) % 4
        return pltpu.make_async_remote_copy(
            src_ref=gwp.at[pl.ds(pl.multiple_of((2 * cx + 1 - mc) * CHUNK, 16), CHUNK)],
            dst_ref=cbuf.at[pl.ds(pl.multiple_of(cx * CHUNK, 16), CHUNK)],
            send_sem=c_ss.at[n], recv_sem=c_rs.at[n],
            device_id=(2 * mx + 1 - mc, ml), device_id_type=MESH,
        )

    for n in (2, 1, 3, 0):
        c_copy(n).start()

    forward_on(2)

    def chip_sum(n, half):
        cx = (mx + n) % 4
        a = gwp[pl.ds(pl.multiple_of((2 * cx + mc) * CHUNK + half * HALFC, 16), HALFC), :]
        b = cbuf[pl.ds(pl.multiple_of(cx * CHUNK + half * HALFC, 16), HALFC), :]
        return a + b

    up = (2 * ((mx + 1) % 4) + mc, ml)
    down = (2 * ((mx + 3) % 4) + mc, ml)

    def x_copy(n, src, dst, to):
        return pltpu.make_async_remote_copy(
            src_ref=src, dst_ref=dst, send_sem=x_ss.at[n], recv_sem=x_rs.at[n],
            device_id=to, device_id_type=MESH,
        )

    c_copy(2).wait()
    xsa[...] = chip_sum(2, 0).astype(BF)
    xsb[...] = chip_sum(2, 1).astype(BF)
    x0 = x_copy(0, xsa, xra, up)
    x0.start()
    x1 = x_copy(1, xsb, xrb, down)
    x1.start()
    forward_on(6)
    c_copy(1).wait()
    xsp[...] = chip_sum(1, 1).astype(BF)
    x2 = x_copy(2, xsp, xrp, up)
    x2.start()
    c_copy(3).wait()
    xsm[...] = chip_sum(3, 0).astype(BF)
    x3 = x_copy(3, xsm, xrm, down)
    x3.start()
    forward_on(1)
    c_copy(0).wait()
    x0.wait()
    xs2p[...] = (chip_sum(1, 0) + xra[...].astype(F32)).astype(BF)
    x4 = x_copy(4, xs2p, xr2p, up)
    x4.start()
    x1.wait()
    xs2m[...] = (chip_sum(3, 1) + xrb[...].astype(F32)).astype(BF)
    x5 = x_copy(5, xs2m, xr2m, down)
    x5.start()

    forward_on(7)
    forward_on(0)
    e2r[pl.ds(mz * 16, 16)] = e2m[pl.ds(mz * 16, 16)]

    @pl.loop(0, 2)
    def _(b):
        rows = pl.ds(pl.multiple_of(b * 256, 256), 256)
        for s in SHIFTS:
            ps = HOLD[s]
            first = FIRST[s] * 128
            part = lax.dot_general(
                gs[pl.ds(pl.multiple_of(s * 512 + b * 256, 256), 256), :],
                wr[first : first + 128 * len(ps), :],
                (((1,), (1,)), ((), ())),
                preferred_element_type=F32,
            )
            for n, p in enumerate(ps):
                piece = part[:, n * 128 : n * 128 + 128]
                if s == 0:
                    gx[rows, p * 128 : p * 128 + 128] = piece
                else:
                    gx[rows, p * 128 : p * 128 + 128] += piece

    @pl.loop(0, 8)
    def _(i):
        halves = []
        for h in range(2):
            rows = pl.ds(pl.multiple_of(i * 64, 64) + 32 * h, 32)
            halves.append(jnp.concatenate([gx[rows, p * 128 : p * 128 + 128] for p in range(8)], axis=0))
        block = jnp.concatenate(halves, axis=1).astype(BF)
        block = jnp.where(i < count, block, jnp.zeros((), BF))
        back_ = dot(permt[...], block).astype(BF)
        at = pl.multiple_of(i * 512, 512)
        gl[pl.ds(at, 256), :] = back_[:, 0:128]
        gl[pl.ds(at + 256, 256), :] = back_[:, 128:256]

    gl_out = pltpu.make_async_copy(gl, gl_h, out_sem.at[0])
    gl_out.start()

    x3.wait()
    x4.wait()
    own[0:HALFC, :] = chip_sum(0, 0) + xrm[...].astype(F32) + xr2p[...].astype(F32)
    x2.wait()
    x5.wait()
    own[HALFC:CHUNK, :] = chip_sum(0, 1) + xrp[...].astype(F32) + xr2m[...].astype(F32)
    lsend[...] = own[...].astype(BF)

    def ly_copy(d):
        to = (my + d) % 4
        return remote(
            lsend.at[pl.ds(pl.multiple_of(to * 112, 16), 112)],
            lrecv.at[pl.ds(pl.multiple_of(my * 112, 16), 112)],
            ly_ss.at[d], ly_rs.at[d], at_y(d),
        )

    for d in (2, 1, 3):
        ly_copy(d).start()
    total = own[pl.ds(pl.multiple_of(my * 112, 16), 112), :]
    for d in (2, 1, 3):
        ly_copy(d).wait()
        came = (my + 4 - d) % 4
        total = total + lrecv[pl.ds(pl.multiple_of(came * 112, 16), 112), :].astype(F32)
    zsend[0:112, :] = total

    def block_for(z):
        return (z + 14 - ms) % 8

    def lz_copy(d):
        c = block_for((mz + d) % 8)
        return remote(
            zsend.at[pl.ds(pl.multiple_of(c * 16, 16), 16)],
            zrecv.at[pl.ds(pl.multiple_of(mz * 16, 16), 16)],
            lz_ss.at[d], lz_rs.at[d], at_z(d),
        )

    mine = block_for(mz)
    for d in FAR_FIRST[:7]:
        @pl.when(block_for((mz + d) % 8) != 7)
        def _():
            lz_copy(d).start()

    def f_copy(d):
        return remote(
            fs, frecv.at[pl.ds(pl.multiple_of((6 - mine) * 16, 16), 16)],
            f_ss.at[d], f_rs.at[d], ((ms + d) % 8, ml),
        )

    @pl.when(mine != 7)
    def _():
        for d in FAR_FIRST[:7]:
            lz_copy(d).wait_recv()
        total = zsend[pl.ds(pl.multiple_of(mine * 16, 16), 16), :]
        for d in range(1, 8):
            total = total + zrecv[pl.ds(pl.multiple_of((mz + d) % 8 * 16, 16), 16), :]
        fs[...] = total

        @pl.loop(1, 8)
        def _(d):
            f_copy(d).start()

        frecv[pl.ds(pl.multiple_of((6 - mine) * 16, 16), 16), :] = fs[...]

    for d in FAR_FIRST[:7]:
        @pl.when(block_for((mz + d) % 8) != 7)
        def _():
            lz_copy(d).wait_send()

    for d in range(1, 8):
        eb_copy(d).wait()

    @pl.loop(0, 8)
    def _(i):
        for d in range(7):
            of[d * 16 : d * 16 + 16, :] = e2r[ids[2, i * 8 + d]]
        of[112:128, :] = jnp.zeros((16, 256), BF)
        rows = pl.ds(pl.multiple_of(i * 64, 64), 64)
        y = e_int[rows, :] + e5[pl.ds(pl.multiple_of(i * 128, 128), 64), :] + dot(facet[...], of[...])
        out[rows, :] = jnp.where(i < count, y, 0.0).astype(BF)

    out_out = pltpu.make_async_copy(out, out_h, out_sem.at[1])
    out_out.start()

    @pl.loop(1, 8)
    def _(d):
        @pl.when((mz + 14 - (ms + 8 - d) % 8) % 8 != 7)
        def _():
            came = (mz + 14 - (ms + 8 - d) % 8) % 8
            remote(
                fs, frecv.at[pl.ds(pl.multiple_of((6 - came) * 16, 16), 16)],
                f_ss.at[d], f_rs.at[d], ((ms + d) % 8, ml),
            ).wait_recv()

    @pl.when(mine != 7)
    def _():
        @pl.loop(1, 8)
        def _(d):
            f_copy(d).wait_send()

    gw[...] = frecv[0:108, :]
    gl_out.wait()
    out_out.wait()


def request_tables(nbr_owner, nbr_slot, counts):
    pad = ((0, 0), (0, 1))
    pick = np.array([code - 1 for code in CODES])
    owners = jnp.pad(nbr_owner[:, pick], pad, constant_values=32).reshape(64)
    blocks = (jnp.pad(nbr_slot[:, pick], pad) * 8 + jnp.arange(8, dtype=jnp.int32)[None, :]).reshape(64)
    n = jnp.arange(64, dtype=jnp.int32)
    rank = jnp.sum((owners[:, None] == owners[None, :]) & (n[None, :] < n[:, None]), axis=1, dtype=jnp.int32)
    place = owners * 4 + rank
    hit = place[None, :] == jnp.arange(128, dtype=jnp.int32)[:, None]
    source = 7 + jnp.sum(jnp.where(hit, n[None, :] - 7, 0), axis=1, dtype=jnp.int32)
    code = 7 + jnp.sum(jnp.where(hit, blocks[None, :] - 7, 0), axis=1, dtype=jnp.int32)
    places = jnp.pad((owners % 8 * 4 + owners // 8) * 4 + rank, (0, 64))
    return jnp.stack([source, code, places, jnp.broadcast_to(counts.reshape(1), (128,))])


def per_device(leaves, counts, nbr_owner, nbr_slot, weight, cotangent):
    ids = request_tables(nbr_owner[0], nbr_slot[0], counts)
    consts = [jnp.asarray(t, BF) for t in tables()]
    vmem = pl.BlockSpec(memory_space=pltpu.VMEM)
    hbm = pl.BlockSpec(memory_space=pl.ANY)
    sems = pltpu.SemaphoreType.DMA
    V = pltpu.VMEM
    out, gl, gw = pl.pallas_call(
        kernel,
        out_shape=(
            jax.ShapeDtypeStruct((512, 256), BF),
            jax.ShapeDtypeStruct((4096, 128), BF),
            jax.ShapeDtypeStruct((108, 256), F32),
        ),
        in_specs=[pl.BlockSpec(memory_space=pltpu.SMEM), vmem] + [hbm] * 11,
        out_specs=(hbm, hbm, vmem),
        scratch_shapes=[
            V((4096, 128), BF), V((512, 256), BF), *[V(t.shape, BF) for t in consts], V((512, 256), BF), V((4096, 128), BF),
            V((3456, 256), BF), V((512, 1024), BF), V((1024, 512), BF), V((1024, 2432), BF),
            V((512, 256), F32), V((1024, 256), F32), V((512, 256), BF), V((8, ROWS, 256), BF), V((64, 16, 256), BF),
            *[V((128, 16, 256), BF) for _ in range(5)],
            V((32, 1, 256), jnp.int32), pltpu.SMEM((32, 1, 256), jnp.int32), V((8, 512, 256), BF),
            V((512, 256), F32), V((4096, 256), BF), V((512, 1024), F32), V((3472, 256), F32),
            V((8 * CHUNK, 256), F32), V((4 * CHUNK, 256), F32),
            *[V((HALFC, 256), BF) for _ in range(12)],
            V((CHUNK, 256), F32), V((CHUNK, 256), BF), V((CHUNK, 256), BF), V((128, 256), F32), V((128, 256), F32),
            V((16, 256), F32), V((128, 256), F32), V((128, 256), BF),
            sems((10,)), sems, sems, sems((2,)), sems((16,)), sems((16,)), sems((8,)), sems((8,)), sems((4,)), sems((4,)),
            sems((32,)), sems((32,)), sems((32,)), sems((32,)), sems((8,)), sems((8,)),
            sems((4,)), sems((4,)), sems((6,)), sems((6,)), sems((4,)), sems((4,)), sems((8,)), sems((8,)),
            sems((8,)), sems((8,)),
        ],
        compiler_params=pltpu.CompilerParams(
            collective_id=0, has_side_effects=True, vmem_limit_bytes=56 * 1024 * 1024
        ),
        cost_estimate=pl.CostEstimate(flops=3 * 10**9, bytes_accessed=5 * 10**6, transcendentals=0),
    )(ids, ids, leaves.reshape(4096, 128), cotangent.reshape(512, 256), weight, *consts)
    return (
        out.reshape(1, 8, 4, 4, 4, 256),
        gl.reshape(1, 8, 8, 8, 8, 128),
        gw,
    )


def solution(mesh):
    six = P("scene", "leaf", None, None, None, None)
    return jax.shard_map(
        per_device,
        mesh=mesh,
        in_specs=(six, P("scene", "leaf"), P("scene", "leaf", None), P("scene", "leaf", None), P(), six),
        out_specs=(six, six, P("leaf", None)),
        check_vma=False,
    )
```

time: 91.5 us -> 82.4 us (0.901)
  Pallas kernels: 79 us -> 69.9 us
    pallas_call x1, Pallas kernels: 79 us -> 69.9 us  [per_device(): pl.pallas_call(kernel, out_shape=(jax.ShapeDtypeStruct((512, 256), BF), j...]
where the time goes in v1:
time: 82.4 us; the launch traced here: 82.2 us
  Pallas kernels  69.9 us (85%)
  local copies, waits for them, and re-layouts  9.26 us (11%)
  other arithmetic  1.63 us (2%)
  between operations  1.34 us (2%)
    pallas_call x1, Pallas kernels, per_device(): pl.pallas_call(kernel, out_shape=(jax.ShapeDtypeStruct((512, 256), BF), j...  69.9 us
    unnamed x5, local copies, waits for them, and re-layouts  2.99 us
    reshape x1, local copies, waits for them, and re-layouts, per_device(): return (out.reshape(1, 8, 4, 4, 4, 256), gl.reshape(1, 8, 8, 8, 8, 128), gw)  1.75 us
    reshape x1, local copies, waits for them, and re-layouts, per_device(): cotangent.reshape(512, 256)  1.72 us

profile of v1, /device:TPU:1, one launch (start us, length us, event | category | flops | bytes accessed | tf_op | source)
XLA Modules:
  0.0 82.2 jit_solution(11396039602598435454)
XLA Ops:
  1.3 0.1 pad.17.clone
  1.4 0.7 pad_clamp_fusion
  2.0 0.7 copy.38
  2.7 0.6 gather_fusion
  3.3 0.1 copy.34
  3.3 0.1 reshape.70
  3.4 0.2 convert_reduce_fusion
  3.6 0.7 copy.37
  4.3 0.6 gather_fusion.1
  4.9 0.1 copy.31
  5.0 0.1 sub.16
  5.1 0.1 select_reduce_fusion.1
  5.2 0.6 add_add_fusion.1.ids.idv
  5.8 1.7 %reshape.73.cot_h = bf16[512,256]{1,0:T(8,128)(2,1)} reshape(bf16[1,8,4,4,4,256]{5,4,3,2,1,0:T(4,128)(2,1)} %param.22) | data formatting | bytes 524288 | tf_op jit(solution)/shard_map/reshape | solution.py:659
  7.5 69.9 %shard_map.184 = (bf16[512,256]{1,0:T(8,128)(2,1)}, bf16[4096,128]{1,0:T(8,128)(2,1)}, f32[108,256]{1,0:T(8,128)}) custom-call(s32[4,128]{1,0:T(4,128)} %add_add_fusion.1.ids.idv, s32[4,128]{1,0:T(4,128)} %add_add_fusion.1.ids.idv, bf16[4096,128]{1,0:T(8,128)(2,1)} %bitcast.27, bf16[512,256]{1,0:T(8,128)(2,1)} %reshape.73.cot_h, bf16[3456,256]{1,0:T(8,128)(2,1)} %w_h.1, ...), custom_call_target="tpu_custom_call" | custom-call | flops 3000000000 | bytes 5000000 | tf_op jit(solution)/shard_map/pallas_call | solution.py:630
  77.5 0.0 copy-start
  77.5 1.8 %reshape.74 = bf16[1,8,4,4,4,256]{5,4,3,2,1,0:T(4,128)(2,1)} reshape(bf16[512,256]{1,0:T(8,128)(2,1)} %get-tuple-element.6) | data formatting | bytes 524288 | tf_op jit(solution)/shard_map/reshape | solution.py:661
  79.3 2.3 %copy.42 = bf16[1,8,8,8,8,128]{5,4,3,2,1,0:T(8,128)(2,1)} copy(bf16[1,8,8,8,8,128]{5,4,3,2,1,0:T(8,128)(2,1)} %bitcast.22) | data formatting | bytes 2097152
  81.5 0.0 copy-done
  81.5 0.6 copy.43
  (6 shorter events, 0.0 us)
Async XLA Ops:
  77.5 4.0 %copy-start = (f32[108,256]{1,0:T(8,128)S(1)}, f32[108,256]{1,0:T(8,128)}, u32[]{:S(2)}) copy-start(f32[108,256]{1,0:T(8,128)} %get-tuple-element.20) | copy-start | bytes 331780

commit v2 on v1

--- a/solution.py
+++ b/solution.py
@@ -106,20 +106,20 @@
 
 
 def kernel(
-    ids, idv, leaves_h, cot_h, w_h, perm_h, permt_h, facet_h, spread_h, gather_h, expand_h, shift_h, back_h,
+    owners, slots, counts, leaves_h, cot_h, w_h, perm_h, permt_h, facet_h, spread_h, gather_h, expand_h, shift_h, back_h,
     out_h, gl_h, gw,
     leaves, cot, perm, permt, facet, spread, gather, expand, shift, back, out, gl,
-    wr, xc, xt, xb, e_int, e5, gcot, ub, t128, e1s, e1r, e2s, e2m, e2r, codes, codes_sm, pick,
+    idv, ids, column, blocks, wr, xc, xt, xb, e_int, e5, gcot, ub, t128, e1s, e1r, e2s, e2m, e2r, codes, codes_sm,
     ghost, gs, gx, gwn, gwp, cbuf, xsa, xsb, xsp, xsm, xs2p, xs2m, xra, xrb, xrp, xrm, xr2p, xr2m,
     own, lsend, lrecv, zsend, zrecv, fs, frecv, of,
-    in_sem, w_sem, sm_sem, out_sem, ag_ss, ag_rs, iz_ss, iz_rs, iy_ss, iy_rs, e1_ss, e1_rs, ea_ss, ea_rs, eb_ss, eb_rs,
+    in_sem, id_sem, w_sem, sm_sem, out_sem, ag_ss, ag_rs, iz_ss, iz_rs, iy_ss, iy_rs, e1_ss, e1_rs, ea_ss, ea_rs, eb_ss, eb_rs,
     c_ss, c_rs, x_ss, x_rs, ly_ss, ly_rs, lz_ss, lz_rs, f_ss, f_rs,
 ):
     ms = lax.axis_index("scene")
     ml = lax.axis_index("leaf")
     my, mz = ml // 8, ml % 8
     mx, mc = ms // 2, ms % 2
-    count = ids[3, 0]
+    count = counts[0, 0]
 
     def remote(src, dst, ss, rs, to):
         return pltpu.make_async_remote_copy(
@@ -162,12 +162,38 @@
     def _(d):
         pl.semaphore_signal(barrier, inc=1, device_id=at_y(d), device_id_type=MESH)
 
+    for n in range(64):
+        i, d = n // 8, n % 8
+        if d < 7:
+            owner, block = owners[CODES[d] - 1, i], slots[CODES[d] - 1, i] * 8 + d
+        else:
+            owner, block = jnp.int32(99), jnp.int32(7)
+        column[n : n + 1, :] = jnp.full((1, 128), owner, jnp.int32)
+        blocks[n : n + 1, :] = jnp.full((1, 128), block, jnp.int32)
+    column[64:128, :] = jnp.full((64, 128), 99, jnp.int32)
+    blocks[64:128, :] = jnp.full((64, 128), 7, jnp.int32)
+    down_n = lax.broadcasted_iota(jnp.int32, (128, 128), 0)
+    along_n = lax.broadcasted_iota(jnp.int32, (128, 128), 1)
+    owner_down = column[...]
+    owner_along = owner_down.T
+    same = jnp.where(owner_down == owner_along, 1, 0)
+    rank_down = jnp.sum(jnp.where(along_n < down_n, same, 0), axis=1, keepdims=True)
+    rank_along = jnp.sum(jnp.where(down_n < along_n, same, 0), axis=0, keepdims=True)
+    hit = owner_down * 4 + rank_down == along_n
+    own_row = owner_along[0:1, :]
+    idv[0:1, :] = 7 + jnp.sum(jnp.where(hit, down_n - 7, 0), axis=0, keepdims=True)
+    idv[1:2, :] = 7 + jnp.sum(jnp.where(hit, blocks[...] - 7, 0), axis=0, keepdims=True)
+    idv[2:3, :] = ((own_row & 7) * 4 + (own_row >> 3)) * 4 + rank_along
+    idv[3:8, :] = jnp.zeros((5, 128), jnp.int32)
+    places = pltpu.make_async_copy(idv, ids, id_sem)
+    places.start()
+
     loads[0].wait()
 
     @pl.loop(0, 8)
     def _(i):
         rows = pl.ds(pl.multiple_of(i * 64, 64), 64)
-        gcot[rows, :] = jnp.where(i < count, cot[rows, :], jnp.zeros((), BF))
+        gcot[rows, :] = jnp.where(i < count, cot[pl.ds(i * 16, 16)].reshape(64, 256), jnp.zeros((), BF))
 
     loads[1].wait()
     ub[mz] = dot(gather[...], gcot[...]).astype(BF)
@@ -318,17 +344,10 @@
     all_sm = pltpu.make_async_copy(codes, codes_sm, sm_sem)
     all_sm.start()
     all_sm.wait()
-    forward_rows(1)
-    forward_rows(2)
-    hop_all(3)
-    serve(5)
-    serve(3)
-    forward_rows(3)
-
     lane = lax.broadcasted_iota(jnp.int32, (1, 256), 1)
     goal = lax.broadcasted_iota(jnp.int32, (512, 256), 0)
 
-    def make_pick(q):
+    def gather_ghosts(q):
         z = (mz + q) % 8
         row = jnp.zeros((1, 256), jnp.int32)
         for y in range(4):
@@ -336,36 +355,41 @@
                 row = jnp.where(lane >> 4 == y * 4 + k, codes_sm[y * 8 + z, 0, 128 + ml * 4 + k], row)
         d = row & 7
         target = (row >> 3) * 64 + jnp.where(d < 3, 16 * d, 36 + 4 * d) + (lane & 15)
-        pick[q] = jnp.where(goal == target, 1.0, 0.0).astype(BF)
-
-    ag_copy(0, 0, 4).wait()
-    ag_copy(1, 1, 4).wait()
-    serve(4)
+        pick = jnp.where(goal == target, 1.0, 0.0).astype(BF)
+        for n in range(1, 4):
+            e1_copy(q, n).wait()
+        part = dot(pick, e1r[pl.ds(z * 16, 16)].reshape(256, 256))
+        if q == 0:
+            ghost[...] = part
+        else:
+            ghost[...] += part
+
+    forward_rows(1)
+    forward_rows(2)
+    forward_rows(3)
+
+    hop_all(3)
+    serve(5)
+    serve(3)
 
     @pl.loop(0, 32)
     def _(r):
         for k in range(4):
             e2s[r * 4 + k] = t128[codes_sm[r, 0, 128 + ml * 4 + k]]
 
+    gather_ghosts(0)
+    gather_ghosts(7)
+    gather_ghosts(1)
+    ag_copy(0, 0, 4).wait()
+    ag_copy(1, 1, 4).wait()
+    serve(4)
     for q in FAR_FIRST:
         for d in range(1, 4):
             ea_copy(q, d).start()
     for z in range(8):
         e2m[pl.ds((z * 4 + my) * 4, 4)] = e2s[pl.ds((my * 8 + z) * 4, 4)]
-
-    @pl.loop(0, 8)
-    def _(q):
-        make_pick(q)
-
-    for q in (0, 7, 1, 6, 2, 5, 3, 4):
-        for d in range(1, 4):
-            e1_copy(q, d).wait()
-        z = (mz + q) % 8
-        part = dot(pick[q], e1r[pl.ds(z * 16, 16)].reshape(256, 256))
-        if q == 0:
-            ghost[...] = part
-        else:
-            ghost[...] += part
+    for q in (6, 2, 5, 3, 4):
+        gather_ghosts(q)
 
     def forward_on(q):
         for d in range(1, 4):
@@ -569,6 +593,7 @@
         def _():
             lz_copy(d).wait_send()
 
+    places.wait()
     for d in range(1, 8):
         eb_copy(d).wait()
 
@@ -579,7 +604,7 @@
         of[112:128, :] = jnp.zeros((16, 256), BF)
         rows = pl.ds(pl.multiple_of(i * 64, 64), 64)
         y = e_int[rows, :] + e5[pl.ds(pl.multiple_of(i * 128, 128), 64), :] + dot(facet[...], of[...])
-        out[rows, :] = jnp.where(i < count, y, 0.0).astype(BF)
+        out[pl.ds(i * 16, 16)] = jnp.where(i < count, y, 0.0).astype(BF).reshape(16, 4, 256)
 
     out_out = pltpu.make_async_copy(out, out_h, out_sem.at[1])
     out_out.start()
@@ -605,23 +630,32 @@
     out_out.wait()
 
 
-def request_tables(nbr_owner, nbr_slot, counts):
-    pad = ((0, 0), (0, 1))
-    pick = np.array([code - 1 for code in CODES])
-    owners = jnp.pad(nbr_owner[:, pick], pad, constant_values=32).reshape(64)
-    blocks = (jnp.pad(nbr_slot[:, pick], pad) * 8 + jnp.arange(8, dtype=jnp.int32)[None, :]).reshape(64)
-    n = jnp.arange(64, dtype=jnp.int32)
-    rank = jnp.sum((owners[:, None] == owners[None, :]) & (n[None, :] < n[:, None]), axis=1, dtype=jnp.int32)
-    place = owners * 4 + rank
-    hit = place[None, :] == jnp.arange(128, dtype=jnp.int32)[:, None]
-    source = 7 + jnp.sum(jnp.where(hit, n[None, :] - 7, 0), axis=1, dtype=jnp.int32)
-    code = 7 + jnp.sum(jnp.where(hit, blocks[None, :] - 7, 0), axis=1, dtype=jnp.int32)
-    places = jnp.pad((owners % 8 * 4 + owners // 8) * 4 + rank, (0, 64))
-    return jnp.stack([source, code, places, jnp.broadcast_to(counts.reshape(1), (128,))])
+def hand_over(*arrays):
+    def copy(*refs):
+        n = len(arrays)
+        held, sem_in, sem_out = refs[2 * n : 3 * n], refs[3 * n], refs[3 * n + 1]
+        into = [pltpu.make_async_copy(refs[k], held[k], sem_in.at[k]) for k in range(n)]
+        onto = [pltpu.make_async_copy(held[k], refs[n + k], sem_out.at[k]) for k in range(n)]
+        for one in into:
+            one.start()
+        for one, two in zip(into, onto):
+            one.wait()
+            two.start()
+        for two in onto:
+            two.wait()
+
+    hbm = pl.BlockSpec(memory_space=pl.ANY)
+    sems = pltpu.SemaphoreType.DMA
+    return pl.pallas_call(
+        copy,
+        out_shape=tuple(jax.ShapeDtypeStruct(a.shape, a.dtype) for a in arrays),
+        in_specs=[hbm] * len(arrays),
+        out_specs=(hbm,) * len(arrays),
+        scratch_shapes=[pltpu.VMEM(a.shape, a.dtype) for a in arrays] + [sems((len(arrays),)), sems((len(arrays),))],
+    )(*arrays)
 
 
 def per_device(leaves, counts, nbr_owner, nbr_slot, weight, cotangent):
-    ids = request_tables(nbr_owner[0], nbr_slot[0], counts)
     consts = [jnp.asarray(t, BF) for t in tables()]
     vmem = pl.BlockSpec(memory_space=pltpu.VMEM)
     hbm = pl.BlockSpec(memory_space=pl.ANY)
@@ -630,24 +664,25 @@
     out, gl, gw = pl.pallas_call(
         kernel,
         out_shape=(
-            jax.ShapeDtypeStruct((512, 256), BF),
+            jax.ShapeDtypeStruct((128, 4, 256), BF),
             jax.ShapeDtypeStruct((4096, 128), BF),
             jax.ShapeDtypeStruct((108, 256), F32),
         ),
-        in_specs=[pl.BlockSpec(memory_space=pltpu.SMEM), vmem] + [hbm] * 11,
+        in_specs=[pl.BlockSpec(memory_space=pltpu.SMEM)] * 3 + [hbm] * 11,
         out_specs=(hbm, hbm, vmem),
         scratch_shapes=[
-            V((4096, 128), BF), V((512, 256), BF), *[V(t.shape, BF) for t in consts], V((512, 256), BF), V((4096, 128), BF),
+            V((4096, 128), BF), V((128, 4, 256), BF), *[V(t.shape, BF) for t in consts], V((128, 4, 256), BF), V((4096, 128), BF),
+            V((8, 128), jnp.int32), pltpu.SMEM((8, 128), jnp.int32), V((128, 128), jnp.int32), V((128, 128), jnp.int32),
             V((3456, 256), BF), V((512, 1024), BF), V((1024, 512), BF), V((1024, 2432), BF),
             V((512, 256), F32), V((1024, 256), F32), V((512, 256), BF), V((8, ROWS, 256), BF), V((64, 16, 256), BF),
             *[V((128, 16, 256), BF) for _ in range(5)],
-            V((32, 1, 256), jnp.int32), pltpu.SMEM((32, 1, 256), jnp.int32), V((8, 512, 256), BF),
+            V((32, 1, 256), jnp.int32), pltpu.SMEM((32, 1, 256), jnp.int32),
             V((512, 256), F32), V((4096, 256), BF), V((512, 1024), F32), V((3472, 256), F32),
             V((8 * CHUNK, 256), F32), V((4 * CHUNK, 256), F32),
             *[V((HALFC, 256), BF) for _ in range(12)],
             V((CHUNK, 256), F32), V((CHUNK, 256), BF), V((CHUNK, 256), BF), V((128, 256), F32), V((128, 256), F32),
             V((16, 256), F32), V((128, 256), F32), V((128, 256), BF),
-            sems((10,)), sems, sems, sems((2,)), sems((16,)), sems((16,)), sems((8,)), sems((8,)), sems((4,)), sems((4,)),
+            sems((10,)), sems, sems, sems, sems((2,)), sems((16,)), sems((16,)), sems((8,)), sems((8,)), sems((4,)), sems((4,)),
             sems((32,)), sems((32,)), sems((32,)), sems((32,)), sems((8,)), sems((8,)),
             sems((4,)), sems((4,)), sems((6,)), sems((6,)), sems((4,)), sems((4,)), sems((8,)), sems((8,)),
             sems((8,)), sems((8,)),
@@ -656,7 +691,8 @@
             collective_id=0, has_side_effects=True, vmem_limit_bytes=56 * 1024 * 1024
         ),
         cost_estimate=pl.CostEstimate(flops=3 * 10**9, bytes_accessed=5 * 10**6, transcendentals=0),
-    )(ids, ids, leaves.reshape(4096, 128), cotangent.reshape(512, 256), weight, *consts)
+    )(nbr_owner[0].T, nbr_slot[0].T, counts, leaves.reshape(4096, 128), cotangent.reshape(128, 4, 256), weight, *consts)
+    out, gl, gw = hand_over(out, gl, gw)
     return (
         out.reshape(1, 8, 4, 4, 4, 256),
         gl.reshape(1, 8, 8, 8, 8, 128),

time: 82.4 us -> 75.7 us (0.919)
  local copies, waits for them, and re-layouts: 9.26 us -> 1.3 us
  Pallas kernels: 69.9 us -> 72.9 us
  other arithmetic: 1.63 us -> 0 us
    reshape x3 -> x0, local copies, waits for them, and re-layouts: 3.55 us -> none  [the longest x1 1.75 us: per_device(): return (out.reshape(1, 8, 4, 4, 4, 256), gl.reshape(1, 8, 8, 8, 8, 128), gw)]
    unnamed x5 -> x0, local copies, waits for them, and re-layouts: 2.99 us -> none
    pallas_call x1 -> x2, Pallas kernels: 69.9 us -> 72.9 us  [the longest x1 70.5 us: per_device(): pl.pallas_call(kernel, out_shape=(jax.ShapeDtypeStruct((128, 4, 256), BF)...]
    squeeze x2 -> x0, local copies, waits for them, and re-layouts: 1.37 us -> none  [per_device(): ids = request_tables(nbr_owner[0], nbr_slot[0], counts)]
    transpose x0 -> x1, local copies, waits for them, and re-layouts: none -> 1.3 us  [per_device(): nbr_slot[0]]
    gather x2 -> x0, local copies, waits for them, and re-layouts: 1.11 us -> none  [the longest x1 0.55 us: request_tables(): owners = jnp.pad(nbr_owner[:, pick], pad, constant_values=32).reshape(64)]
where the time goes in v2:
time: 75.7 us; the launch traced here: 75.5 us
  Pallas kernels  72.9 us (96%)
  local copies, waits for them, and re-layouts  1.3 us (2%)
  between operations  1.29 us (2%)
    pallas_call x1, Pallas kernels, per_device(): pl.pallas_call(kernel, out_shape=(jax.ShapeDtypeStruct((128, 4, 256), BF)...  70.5 us
    pallas_call x1, Pallas kernels, hand_over(): pl.pallas_call(copy, out_shape=tuple((jax.ShapeDtypeStruct(a.shape, a.dty...  2.36 us

profile of v2, /device:TPU:1, one launch (start us, length us, event | category | flops | bytes accessed | tf_op | source)
XLA Modules:
  0.0 75.5 jit_solution(16744539842188249460)
XLA Ops:
  1.3 1.3 %copy_bitcast_fusion = (s32[7,8]{1,0:T(8,128)}, s32[7,8]{1,0:T(8,128)}) fusion(s32[1,8,7]{1,0,2:T(1,128)} %param.17, s32[1,8,7]{1,0,2:T(1,128)} %param.16), kind=kLoop, calls=%fused_computation | loop fusion | bytes 896 | tf_op jit(solution)/shard_map/transpose | solution.py:694
  2.6 70.5 %shard_map.157 = (bf16[128,4,256]{2,1,0:T(4,128)(2,1)}, bf16[4096,128]{1,0:T(8,128)(2,1)}, f32[108,256]{1,0:T(8,128)}) custom-call(s32[7,8]{1,0:T(8,128)} %get-tuple-element.16.owners, s32[7,8]{1,0:T(8,128)} %get-tuple-element.15.slots, s32[1,1]{1,0:T(1,128)S(6)} %copy.25.counts, bf16[4096,128]{1,0:T(8,128)(2,1)} %bitcast.14, bf16[128,4,256]{2,1,0:T(4,128)(2,1)} %bitcast.16, ...), custom_call_target="tpu_custom_call" | custom-call | flops 3000000000 | bytes 5000000 | tf_op jit(solution)/shard_map/pallas_call | solution.py:664
  73.1 2.4 %shard_map.158 = (bf16[128,4,256]{2,1,0:T(4,128)(2,1)}, bf16[4096,128]{1,0:T(8,128)(2,1)}, f32[108,256]{1,0:T(8,128)}) custom-call(bf16[128,4,256]{2,1,0:T(4,128)(2,1)} %get-tuple-element.9.refs_0_, bf16[4096,128]{1,0:T(8,128)(2,1)} %get-tuple-element.10.refs_1_, f32[108,256]{1,0:T(8,128)} %get-tuple-element.11.refs_2_), custom_call_target="tpu_custom_call" | custom-call | tf_op jit(solution)/shard_map/pallas_call | solution.py:649

commit v3 on v2

--- a/solution.py
+++ b/solution.py
@@ -162,6 +162,36 @@
     def _(d):
         pl.semaphore_signal(barrier, inc=1, device_id=at_y(d), device_id_type=MESH)
 
+    loads[0].wait()
+
+    @pl.loop(0, 8)
+    def _(i):
+        rows = pl.ds(pl.multiple_of(i * 64, 64), 64)
+        gcot[rows, :] = jnp.where(i < count, cot[pl.ds(i * 16, 16)].reshape(64, 256), jnp.zeros((), BF))
+
+    loads[1].wait()
+    ub[mz] = dot(gather[...], gcot[...]).astype(BF)
+    pl.semaphore_wait(barrier, 17)
+
+    halves = (pl.ds(0, PART), pl.ds(PART, ROWS - PART))
+
+    def ag_copy(way, half, hop):
+        origin = (mz + 8 - (hop - 1)) % 8 if way == 0 else (mz + hop - 1) % 8
+        block = ub.at[origin, halves[half]]
+        n = (way * 2 + half) * 4 + hop - 1
+        return remote(block, block, ag_ss.at[n], ag_rs.at[n], at_z(1 if way == 0 else 7))
+
+    def iz_copy(d):
+        return remote(codes.at[ml], codes.at[ml], iz_ss.at[d], iz_rs.at[d], at_z(d))
+
+    def iy_copy(d):
+        group = codes.at[pl.ds(my * 8, 8)]
+        return remote(group, group, iy_ss.at[d], iy_rs.at[d], at_y(d))
+
+    for way in range(2):
+        for half in (way, 1 - way):
+            ag_copy(way, half, 1).start()
+
     for n in range(64):
         i, d = n // 8, n % 8
         if d < 7:
@@ -188,18 +218,23 @@
     places = pltpu.make_async_copy(idv, ids, id_sem)
     places.start()
 
-    loads[0].wait()
-
-    @pl.loop(0, 8)
-    def _(i):
-        rows = pl.ds(pl.multiple_of(i * 64, 64), 64)
-        gcot[rows, :] = jnp.where(i < count, cot[pl.ds(i * 16, 16)].reshape(64, 256), jnp.zeros((), BF))
-
-    loads[1].wait()
-    ub[mz] = dot(gather[...], gcot[...]).astype(BF)
     codes[ml, :, 0:128] = idv[0:1, :]
     codes[ml, :, 128:256] = idv[1:2, :]
 
+    @pl.loop(1, 8)
+    def _(d):
+        iz_copy(d).start()
+
+    def hop_done(way, half, hop):
+        ag_copy(way, half, hop).wait()
+        if hop < (4 if half == way else 3):
+            ag_copy(way, half, hop + 1).start()
+
+    def hop_part(part, hop):
+        hop_done(0, part, hop)
+        hop_done(1, 1 - part, hop)
+
+    hop_part(0, 1)
     loads[2].wait()
     loads[3].wait()
 
@@ -215,31 +250,7 @@
                     p * 32 : p * 32 + 32, h * 128 : h * 128 + 128
                 ]
 
-    pl.semaphore_wait(barrier, 17)
-
-    halves = (pl.ds(0, PART), pl.ds(PART, ROWS - PART))
-
-    def ag_copy(way, half, hop):
-        origin = (mz + 8 - (hop - 1)) % 8 if way == 0 else (mz + hop - 1) % 8
-        block = ub.at[origin, halves[half]]
-        n = (way * 2 + half) * 4 + hop - 1
-        return remote(block, block, ag_ss.at[n], ag_rs.at[n], at_z(1 if way == 0 else 7))
-
-    def iz_copy(d):
-        return remote(codes.at[ml], codes.at[ml], iz_ss.at[d], iz_rs.at[d], at_z(d))
-
-    def iy_copy(d):
-        group = codes.at[pl.ds(my * 8, 8)]
-        return remote(group, group, iy_ss.at[d], iy_rs.at[d], at_y(d))
-
-    @pl.loop(1, 8)
-    def _(d):
-        iz_copy(d).start()
-
-    for way in range(2):
-        for half in (way, 1 - way):
-            ag_copy(way, half, 1).start()
-
+    hop_part(1, 1)
     for p in range(8):
         xt[p * 128 : p * 128 + 128, :] = xc[:, p * 128 : p * 128 + 128].T
 
@@ -252,7 +263,6 @@
     group = pl.ds(my * 8, 8)
     to_sm = pltpu.make_async_copy(codes.at[group], codes_sm.at[group], sm_sem)
     to_sm.start()
-    to_sm.wait()
 
     for load in loads[4:]:
         load.wait()
@@ -280,14 +290,6 @@
         for d in range(1, 4):
             e1_copy(q, d).start()
         e1r[pl.ds((z * 4 + my) * 4, 4)] = e1s[pl.ds((z * 4 + my) * 4, 4)]
-
-    serve(0)
-    pltpu.make_async_copy(w_h, wr, w_sem).wait()
-
-    @pl.loop(0, 2)
-    def _(b):
-        rows = pl.ds(pl.multiple_of(b * 256, 256), 256)
-        e_int[rows, :] = dot(xc[rows, :], wr[0:1024, :])
 
     def forward_shift(g):
         rows = pl.ds(g * 256, 256)
@@ -306,16 +308,6 @@
             t64 = e5[pl.ds(i * 128 + 64, 64), :].astype(BF)
             t128[pl.ds(i * 8, 8)] = dot(spread[...], t64).astype(BF).reshape(8, 16, 256)
 
-    def hop_done(way, half, hop):
-        ag_copy(way, half, hop).wait()
-        if hop < (4 if half == way else 3):
-            ag_copy(way, half, hop + 1).start()
-
-    def hop_all(hop):
-        for half in (0, 1):
-            hop_done(0, half, hop)
-            hop_done(1, 1 - half, hop)
-
     def ea_copy(q, d):
         z = (mz + q) % 8
         to = (my + d) % 4
@@ -330,20 +322,6 @@
             e2m.at[pl.ds(z * 16, 16)], e2r.at[pl.ds(mz * 16, 16)], eb_ss.at[d], eb_rs.at[d], at_z(d)
         )
 
-    forward_shift(0)
-    hop_all(1)
-    serve(7)
-    serve(1)
-    forward_shift(1)
-    forward_rows(0)
-    hop_all(2)
-    serve(6)
-    serve(2)
-    for d in range(1, 4):
-        iy_copy(d).wait()
-    all_sm = pltpu.make_async_copy(codes, codes_sm, sm_sem)
-    all_sm.start()
-    all_sm.wait()
     lane = lax.broadcasted_iota(jnp.int32, (1, 256), 1)
     goal = lax.broadcasted_iota(jnp.int32, (512, 256), 0)
 
@@ -364,31 +342,45 @@
         else:
             ghost[...] += part
 
+    hop_part(0, 2)
+    to_sm.wait()
+    serve(0)
+    hop_part(1, 2)
+    serve(7)
+    serve(1)
+    hop_part(0, 3)
+    for d in range(1, 4):
+        iy_copy(d).wait()
+    all_sm = pltpu.make_async_copy(codes, codes_sm, sm_sem)
+    all_sm.start()
+    pltpu.make_async_copy(w_h, wr, w_sem).wait()
+    forward_shift(0)
+    hop_part(1, 3)
+    all_sm.wait()
+    serve(6)
+    serve(2)
+    serve(5)
+    serve(3)
+    forward_shift(1)
+    ag_copy(0, 0, 4).wait()
+    ag_copy(1, 1, 4).wait()
+    serve(4)
+    forward_rows(0)
     forward_rows(1)
     forward_rows(2)
     forward_rows(3)
-
-    hop_all(3)
-    serve(5)
-    serve(3)
 
     @pl.loop(0, 32)
     def _(r):
         for k in range(4):
             e2s[r * 4 + k] = t128[codes_sm[r, 0, 128 + ml * 4 + k]]
 
-    gather_ghosts(0)
-    gather_ghosts(7)
-    gather_ghosts(1)
-    ag_copy(0, 0, 4).wait()
-    ag_copy(1, 1, 4).wait()
-    serve(4)
     for q in FAR_FIRST:
         for d in range(1, 4):
             ea_copy(q, d).start()
     for z in range(8):
         e2m[pl.ds((z * 4 + my) * 4, 4)] = e2s[pl.ds((my * 8 + z) * 4, 4)]
-    for q in (6, 2, 5, 3, 4):
+    for q in (0, 7, 1, 6, 2, 5, 3, 4):
         gather_ghosts(q)
 
     def forward_on(q):
@@ -524,6 +516,11 @@
 
     gl_out = pltpu.make_async_copy(gl, gl_h, out_sem.at[0])
     gl_out.start()
+
+    @pl.loop(0, 2)
+    def _(b):
+        rows = pl.ds(pl.multiple_of(b * 256, 256), 256)
+        e_int[rows, :] = dot(xc[rows, :], wr[0:1024, :])
 
     x3.wait()
     x4.wait()

time: 75.7 us -> 74.1 us (0.979)
  Pallas kernels: 72.9 us -> 71.4 us
    pallas_call x1, Pallas kernels: 70.5 us -> 69 us  [per_device(): pl.pallas_call(kernel, out_shape=(jax.ShapeDtypeStruct((128, 4, 256), BF)...]
where the time goes in v3:
time: 74.1 us; the launch traced here: 73.9 us
  Pallas kernels  71.4 us (96%)
  local copies, waits for them, and re-layouts  1.3 us (2%)
  between operations  1.29 us (2%)
    pallas_call x1, Pallas kernels, per_device(): pl.pallas_call(kernel, out_shape=(jax.ShapeDtypeStruct((128, 4, 256), BF)...  69 us
    pallas_call x1, Pallas kernels, hand_over(): pl.pallas_call(copy, out_shape=tuple((jax.ShapeDtypeStruct(a.shape, a.dty...  2.36 us

profile of v3, /device:TPU:1, one launch (start us, length us, event | category | flops | bytes accessed | tf_op | source)
XLA Modules:
  0.0 73.9 jit_solution(8549637280091167419)
XLA Ops:
  1.3 1.3 %copy_bitcast_fusion = (s32[7,8]{1,0:T(8,128)}, s32[7,8]{1,0:T(8,128)}) fusion(s32[1,8,7]{1,0,2:T(1,128)} %param.17, s32[1,8,7]{1,0,2:T(1,128)} %param.16), kind=kLoop, calls=%fused_computation | loop fusion | bytes 896 | tf_op jit(solution)/shard_map/transpose | solution.py:691
  2.6 69.0 %shard_map.157 = (bf16[128,4,256]{2,1,0:T(4,128)(2,1)}, bf16[4096,128]{1,0:T(8,128)(2,1)}, f32[108,256]{1,0:T(8,128)}) custom-call(s32[7,8]{1,0:T(8,128)} %get-tuple-element.16.owners, s32[7,8]{1,0:T(8,128)} %get-tuple-element.15.slots, s32[1,1]{1,0:T(1,128)S(6)} %copy.25.counts, bf16[4096,128]{1,0:T(8,128)(2,1)} %bitcast.14, bf16[128,4,256]{2,1,0:T(4,128)(2,1)} %bitcast.16, ...), custom_call_target="tpu_custom_call" | custom-call | flops 3000000000 | bytes 5000000 | tf_op jit(solution)/shard_map/pallas_call | solution.py:661
  71.6 2.4 %shard_map.158 = (bf16[128,4,256]{2,1,0:T(4,128)(2,1)}, bf16[4096,128]{1,0:T(8,128)(2,1)}, f32[108,256]{1,0:T(8,128)}) custom-call(bf16[128,4,256]{2,1,0:T(4,128)(2,1)} %get-tuple-element.9.refs_0_, bf16[4096,128]{1,0:T(8,128)(2,1)} %get-tuple-element.10.refs_1_, f32[108,256]{1,0:T(8,128)} %get-tuple-element.11.refs_2_), custom_call_target="tpu_custom_call" | custom-call | tf_op jit(solution)/shard_map/pallas_call | solution.py:646

commit v4 on v3

--- a/solution.py
+++ b/solution.py
@@ -345,28 +345,28 @@
     hop_part(0, 2)
     to_sm.wait()
     serve(0)
+    pltpu.make_async_copy(w_h, wr, w_sem).wait()
+    forward_shift(0)
     hop_part(1, 2)
     serve(7)
     serve(1)
+    forward_shift(1)
     hop_part(0, 3)
     for d in range(1, 4):
         iy_copy(d).wait()
     all_sm = pltpu.make_async_copy(codes, codes_sm, sm_sem)
     all_sm.start()
-    pltpu.make_async_copy(w_h, wr, w_sem).wait()
-    forward_shift(0)
+    forward_rows(0)
     hop_part(1, 3)
     all_sm.wait()
     serve(6)
     serve(2)
     serve(5)
     serve(3)
-    forward_shift(1)
+    forward_rows(1)
     ag_copy(0, 0, 4).wait()
     ag_copy(1, 1, 4).wait()
     serve(4)
-    forward_rows(0)
-    forward_rows(1)
     forward_rows(2)
     forward_rows(3)
 

time: 74.1 us -> 74.4 us (level)
  no operation moved by 1% of the time
where the time goes in v4:
time: 74.4 us; the launch traced here: 74.2 us
  Pallas kernels  71.6 us (96%)
  local copies, waits for them, and re-layouts  1.3 us (2%)
  between operations  1.29 us (2%)
    pallas_call x1, Pallas kernels, per_device(): pl.pallas_call(kernel, out_shape=(jax.ShapeDtypeStruct((128, 4, 256), BF)...  69.2 us
    pallas_call x1, Pallas kernels, hand_over(): pl.pallas_call(copy, out_shape=tuple((jax.ShapeDtypeStruct(a.shape, a.dty...  2.36 us

profile of v4, /device:TPU:1, one launch (start us, length us, event | category | flops | bytes accessed | tf_op | source)
XLA Modules:
  0.0 74.2 jit_solution(3288660603746623972)
XLA Ops:
  1.3 1.3 %copy_bitcast_fusion = (s32[7,8]{1,0:T(8,128)}, s32[7,8]{1,0:T(8,128)}) fusion(s32[1,8,7]{1,0,2:T(1,128)} %param.17, s32[1,8,7]{1,0,2:T(1,128)} %param.16), kind=kLoop, calls=%fused_computation | loop fusion | bytes 896 | tf_op jit(solution)/shard_map/transpose | solution.py:691
  2.6 69.2 %shard_map.157 = (bf16[128,4,256]{2,1,0:T(4,128)(2,1)}, bf16[4096,128]{1,0:T(8,128)(2,1)}, f32[108,256]{1,0:T(8,128)}) custom-call(s32[7,8]{1,0:T(8,128)} %get-tuple-element.16.owners, s32[7,8]{1,0:T(8,128)} %get-tuple-element.15.slots, s32[1,1]{1,0:T(1,128)S(6)} %copy.25.counts, bf16[4096,128]{1,0:T(8,128)(2,1)} %bitcast.14, bf16[128,4,256]{2,1,0:T(4,128)(2,1)} %bitcast.16, ...), custom_call_target="tpu_custom_call" | custom-call | flops 3000000000 | bytes 5000000 | tf_op jit(solution)/shard_map/pallas_call | solution.py:661
  71.8 2.4 %shard_map.158 = (bf16[128,4,256]{2,1,0:T(4,128)(2,1)}, bf16[4096,128]{1,0:T(8,128)(2,1)}, f32[108,256]{1,0:T(8,128)}) custom-call(bf16[128,4,256]{2,1,0:T(4,128)(2,1)} %get-tuple-element.9.refs_0_, bf16[4096,128]{1,0:T(8,128)(2,1)} %get-tuple-element.10.refs_1_, f32[108,256]{1,0:T(8,128)} %get-tuple-element.11.refs_2_), custom_call_target="tpu_custom_call" | custom-call | tf_op jit(solution)/shard_map/pallas_call | solution.py:646
